TPU v7x, 32 devices: a whole 2x2x4 slice. The times are simulated.
32 devices in a mesh: table: 2 (over x), image: 16 (over z, y, core).
Axes of the slice: x: 2, y: 2, z: 4, core: 2. Of those that a mesh axis runs over, the one named last changes fastest.
Arguments:
- traces: bfloat16 [512, 1920], P(('table', 'image')), may hold values from -6 to 6
- aperture: int32 [512, 4], P(('table', 'image')), may hold values from 0 to 15, all different within a row; in each aligned block of 16 rows (0 to 15, 16 to 31, ...) at most 8 rows name the same one
- bucket: int32 [512], P(('table', 'image')), may hold values from 0 to 3
- table_node: int32 [512, 4], P(('table', 'image')), may hold values from 0 to 15
- entry_gain: bfloat16 [512, 4], P(('table', 'image')), may hold values from 0.5 to 2
- travel: float32 [16, 16, 1024], P('image', None, 'table'), may hold values from 1 to 1918
- spread: float32 [16, 16, 1024], P('image', None, 'table'), may hold values from 0.1 to 1
Outputs:
- image: float32 [16, 1024], P('image', 'table')
Inputs may be any that keep to these rules, and one draw needn't show every extreme that they name: `aperture`: each trace names 4 different tiles. Among the 16 traces of one device at most 8 name the same tile, and in every draw some tile is named by exactly 8 of them.
All inputs are finite; a program needn't handle non-finite values.
Results may differ from a plain program's by a relative error of at most 0.0024.
Values may be sent and summed in bfloat16 or wider, within the bound.
A program may use at most 128 MiB of HBM per device.

v0:
```python
import functools
import math

import jax
import jax.numpy as jnp
from jax import lax
from jax.experimental import pallas as pl
from jax.experimental.pallas import tpu as pltpu
from jax.sharding import PartitionSpec as P

LANES = 128
FILTERS = 4
MAX_LAG = 7
MESH = pl.DeviceIdType.MESH


def split_axis(count):
    if count == 16:
        return (4, 2, 2)
    root = math.isqrt(count)
    if root * root == count:
        return (root, root, 1)
    return (count, 1, 1)


def peers(size, at):
    found = []
    for step in range(1, size):
        if size & (size - 1):
            found.append(lax.rem(at + step, size))
            continue
        to, bit = at, 1
        while bit <= step:
            if step & bit:
                to = to + bit * (1 - 2 * lax.rem(to // bit, 2))
            bit *= 2
        found.append(to)
    return found


def eye_column(row, count):
    across = lax.broadcasted_iota(jnp.int32, (count, count), 1)
    down = lax.broadcasted_iota(jnp.int32, (count, count), 0)
    return jnp.sum(jnp.where(across == down, row, 0.0), axis=1, keepdims=True)


def selection(aperture, bucket, node, gain, nodes, half):
    count = aperture.shape[1]
    lane = lax.broadcasted_iota(jnp.int32, (count, 2 * half), 1)
    low = lane < half
    tile = jnp.where(low, lane, lane - half).astype(jnp.float32)
    offset = eye_column(bucket.astype(jnp.float32) * nodes, count)
    total = jnp.zeros((count, 2 * half), jnp.float32)
    for a in range(aperture.shape[0]):
        named = eye_column(aperture[a : a + 1].astype(jnp.float32), count)
        row = eye_column(node[a : a + 1].astype(jnp.float32), count) + offset
        weight = eye_column(gain[a : a + 1].astype(jnp.float32), count)
        total = total + jnp.where(named == tile, jnp.where(low, weight, row), 0.0)
    return total


def triangle(bucket, lag):
    half = 2 + 2 * bucket
    return max(half - lag, 0) / (half * half)


def partial_image(stack, upper, travel, spread):
    floor_value = jnp.floor(travel)
    fraction = travel - floor_value
    lower = floor_value.astype(jnp.int32)
    chunk = lax.shift_right_logical(lower, 7)
    inner = jnp.bitwise_and(lower, LANES - 1)
    pieces = []
    for c in range(travel.shape[1] // LANES):
        cells = slice(c * LANES, (c + 1) * LANES)
        here, within = chunk[:, cells], inner[:, cells]
        low = jnp.zeros(here.shape, jnp.float32)
        high = jnp.zeros(here.shape, jnp.float32)
        for k in range(stack.shape[1] // LANES):
            samples = slice(k * LANES, (k + 1) * LANES)
            mine = here == k
            picked = jnp.take_along_axis(stack[:, samples], within, axis=1, mode="promise_in_bounds")
            above = jnp.take_along_axis(upper[:, samples], within, axis=1, mode="promise_in_bounds")
            low = jnp.where(mine, picked, low)
            high = jnp.where(mine, above, high)
        part = fraction[:, cells]
        value = spread[:, cells] * ((1.0 - part) * low + part * high)
        pieces.append(jnp.sum(value, axis=0, keepdims=True))
    return jnp.concatenate(pieces, axis=1)


def kernel(
    sizes, groups, half, scale,
    aperture_hbm, bucket_hbm, node_hbm, gain_hbm, traces_ref, travel_ref, spread_ref,
    out_ref,
    aperture_ref, bucket_ref, node_ref, gain_ref,
    blocks, travels, spreads, parts, outgoing, total_ref,
    load_sem, send_sem, recv_sem, table_send, table_recv, part_send, part_recv,
):
    size_z, size_y, size_c = sizes
    me = lax.axis_index("image")
    group = lax.axis_index("table")
    z = me // (size_y * size_c)
    y = lax.rem(me // size_c, size_y)
    core = lax.rem(me, size_c)
    count, samples = traces_ref.shape
    nodes = travel_ref.shape[0]
    cells = travel_ref.shape[1]

    def index(at_z, at_y, at_c):
        return (at_z * size_y + at_y) * size_c + at_c

    home = (z * size_c + core) * size_y + y
    loads = [
        pltpu.make_async_copy(source, landing, load_sem.at[k])
        for k, (source, landing) in enumerate((
            (aperture_hbm, aperture_ref), (bucket_hbm, bucket_ref), (node_hbm, node_ref), (gain_hbm, gain_ref),
            (traces_ref, blocks.at[home, :, pl.ds(0, samples)]),
            (travel_ref, travels.at[group]), (spread_ref, spreads.at[group]),
        ))
    ]
    for load in loads:
        load.start()

    def place(at_z, at_y, at_c):
        return (at_z * size_c + at_c) * size_y + at_y

    line_z, line_y, line_c = peers(size_z, z), peers(size_y, y), peers(size_c, core)
    others = [lax.rem(group + r, groups) for r in range(1, groups)]

    barrier = pltpu.get_barrier_semaphore()
    if size_z == 4:
        line_z = [line_z[0], line_z[2], line_z[1]]
    partners = [(group, index(to, y, core)) for to in line_z]
    partners += [(group, index(z, to, core)) for to in line_y]
    partners += [(group, index(z, y, to)) for to in line_c]
    partners += [(other, me) for other in others]
    for partner in partners:
        pl.semaphore_signal(barrier, inc=1, device_id=partner, device_id_type=MESH)

    with jax.named_scope("selection"):
        for load in loads[:4]:
            load.wait()
        blocks[home, :, samples:] = selection(
            aperture_ref[...], bucket_ref[...], node_ref[...], gain_ref[...], nodes, half
        ).astype(jnp.bfloat16)
        loads[4].wait()

    with jax.named_scope("entry_barrier"):
        pl.semaphore_wait(barrier, len(partners))

    started = []

    def block_copy(slot, lane, to):
        return pltpu.make_async_remote_copy(
            src_ref=blocks.at[slot],
            dst_ref=blocks.at[slot],
            send_sem=send_sem.at[lane, slot],
            recv_sem=recv_sem.at[slot],
            device_id=(group, to),
            device_id_type=MESH,
        )

    def send(slot, lane, to):
        copy = block_copy(slot, lane, to)
        copy.start()
        started.append(copy)

    def receive(slot, source):
        block_copy(slot, 0, source).wait_recv()

    def line_copy(at_z, at_c, lane, to):
        first = place(at_z, 0, at_c)
        return pltpu.make_async_remote_copy(
            src_ref=blocks.at[pl.ds(first, size_y)],
            dst_ref=blocks.at[pl.ds(first, size_y)],
            send_sem=send_sem.at[lane, first],
            recv_sem=recv_sem.at[first],
            device_id=(group, to),
            device_id_type=MESH,
        )

    first_y, first_c = size_z - 1, size_z + size_y - 2

    def send_y(slot):
        for k, to in enumerate(line_y):
            send(slot, first_y + k, index(z, to, core))

    send_y(home)
    for k, to in enumerate(line_z):
        send(home, k, index(to, y, core))
    table_copies = []
    for r, other in enumerate(others):
        for which, (source, landing) in enumerate(((travel_ref, travels), (spread_ref, spreads))):
            copy = pltpu.make_async_remote_copy(
                src_ref=source,
                dst_ref=landing.at[group],
                send_sem=table_send.at[which, r],
                recv_sem=table_recv.at[which, group],
                device_id=(other, me),
                device_id_type=MESH,
            )
            copy.start()
            table_copies.append(copy)

    plane = size_y * size_c
    total = plane * count

    def add_plane(at_z, first):
        mine = pl.ds(at_z * plane, plane)
        chosen = blocks[mine, :, samples:].reshape(total, 2 * half).astype(jnp.float32)
        lane = lax.broadcasted_iota(jnp.int32, (1, 2 * half), 1)
        weight = jnp.sum(jnp.where(lane == me, chosen, 0.0), axis=1, keepdims=True)
        row = jnp.sum(jnp.where(lane == me + half, chosen, 0.0), axis=1, keepdims=True)
        rows = lax.broadcasted_iota(jnp.int32, (1, FILTERS * nodes), 1).astype(jnp.float32)
        member = jnp.where(row == rows, weight, 0.0).astype(jnp.bfloat16)
        added = lax.dot_general(
            member,
            blocks[mine, :, :samples].reshape(total, samples),
            (((0,), (0,)), ((), ())),
            preferred_element_type=jnp.float32,
        )
        if first:
            total_ref[...] = added
        else:
            total_ref[...] += added

    def from_z(at_z):
        slot = place(at_z, y, core)
        receive(slot, index(at_z, y, core))
        send_y(slot)

    def from_y(at_z):
        for at_y in line_y:
            receive(place(at_z, at_y, core), index(z, at_y, core))
        for k, to in enumerate(line_c):
            copy = line_copy(at_z, core, first_c + k, index(z, y, to))
            copy.start()
            started.append(copy)

    def from_c(at_z, first):
        for at_c in line_c:
            line_copy(at_z, at_c, 0, index(z, y, at_c)).wait_recv()
        add_plane(at_z, first)

    planes = [z, *line_z]
    for k in range(size_z + 2):
        if 1 <= k < size_z:
            from_z(planes[k])
        if 1 <= k <= size_z:
            from_y(planes[k - 1])
        if k >= 2:
            from_c(planes[k - 2], k == 2)
    stacked = total_ref[...]
    with jax.named_scope("triangle_filter"):
        width = samples + LANES
        stacked = jnp.concatenate([stacked, jnp.zeros((FILTERS * nodes, LANES), jnp.float32)], axis=1)
        by_bucket = [stacked[b * nodes : (b + 1) * nodes] for b in range(FILTERS)]
        stack = None
        for lag in range(MAX_LAG + 1):
            mixed = None
            for b in range(FILTERS):
                if (level := triangle(b, lag)) > 0:
                    term = by_bucket[b] * level
                    mixed = term if mixed is None else mixed + term
            if lag == 0:
                stack = mixed
            else:
                stack = stack + (pltpu.roll(mixed, lag, 1) + pltpu.roll(mixed, width - lag, 1))
        upper = pltpu.roll(stack, width - 1, 1)[:, :samples]
        stack = stack[:, :samples]

    with jax.named_scope("other_image"):
        part_copies = []
        for r, other in enumerate(others):
            for which, landing in enumerate((travels, spreads)):
                pltpu.make_async_remote_copy(
                    src_ref=landing.at[other],
                    dst_ref=landing.at[other],
                    send_sem=table_send.at[which, r],
                    recv_sem=table_recv.at[which, other],
                    device_id=(other, me),
                    device_id_type=MESH,
                ).wait_recv()
            outgoing[r] = partial_image(stack, upper, travels[other], spreads[other])
            copy = pltpu.make_async_remote_copy(
                src_ref=outgoing.at[r],
                dst_ref=parts.at[group],
                send_sem=part_send.at[r],
                recv_sem=part_recv.at[group],
                device_id=(other, me),
                device_id_type=MESH,
            )
            copy.start()
            part_copies.append(copy)
    with jax.named_scope("own_image"):
        for load in loads[5:]:
            load.wait()
        image = partial_image(stack, upper, travels[group], spreads[group])
    with jax.named_scope("last_waits"):
        for copy in started:
            copy.wait_send()
        for copy in table_copies:
            copy.wait_send()
        for r, other in enumerate(others):
            pltpu.make_async_remote_copy(
                src_ref=outgoing.at[r],
                dst_ref=parts.at[other],
                send_sem=part_send.at[r],
                recv_sem=part_recv.at[other],
                device_id=(other, me),
                device_id_type=MESH,
            ).wait_recv()
            image = image + parts[other]
        for copy in part_copies:
            copy.wait_send()
    out_ref[...] = image * scale


def per_device(traces, aperture, bucket, table_node, entry_gain, travel, spread):
    tiles = lax.axis_size("image")
    groups = lax.axis_size("table")
    count, samples = traces.shape
    nodes, cells = travel.shape[1], travel.shape[2]
    half = -(-tiles // (LANES // 2)) * (LANES // 2)
    sizes = split_axis(tiles)
    scale = 1.0 / math.sqrt(count * groups * aperture.shape[1])
    vmem = pl.BlockSpec(memory_space=pltpu.VMEM)
    whole = pl.BlockSpec(memory_space=pl.ANY)
    return pl.pallas_call(
        functools.partial(kernel, sizes, groups, half, scale),
        out_shape=jax.ShapeDtypeStruct((1, cells), jnp.float32),
        in_specs=[whole] * 7,
        out_specs=vmem,
        scratch_shapes=[
            pltpu.VMEM(aperture.shape[::-1], jnp.int32),
            pltpu.VMEM((1, count), jnp.int32),
            pltpu.VMEM(table_node.shape[::-1], jnp.int32),
            pltpu.VMEM(entry_gain.shape[::-1], jnp.bfloat16),
            pltpu.VMEM((tiles, count, samples + 2 * half), jnp.bfloat16),
            pltpu.VMEM((groups, nodes, cells), jnp.float32),
            pltpu.VMEM((groups, nodes, cells), jnp.float32),
            pltpu.VMEM((groups, 1, cells), jnp.float32),
            pltpu.VMEM((max(groups - 1, 1), 1, cells), jnp.float32),
            pltpu.VMEM((FILTERS * nodes, samples), jnp.float32),
            pltpu.SemaphoreType.DMA((7,)),
            pltpu.SemaphoreType.DMA((max(sum(sizes) - 3, 1), tiles)),
            pltpu.SemaphoreType.DMA((tiles,)),
            pltpu.SemaphoreType.DMA((2, max(groups - 1, 1))),
            pltpu.SemaphoreType.DMA((2, groups)),
            pltpu.SemaphoreType.DMA((max(groups - 1, 1),)),
            pltpu.SemaphoreType.DMA((groups,)),
        ],
        compiler_params=pltpu.CompilerParams(
            collective_id=0, has_side_effects=True, vmem_limit_bytes=56 * 1024 * 1024
        ),
        cost_estimate=pl.CostEstimate(flops=10**8, bytes_accessed=10**6, transcendentals=0),
    )(aperture.T, bucket.reshape(1, count), table_node.T, entry_gain.T, traces, travel[0], spread[0])


def solution(mesh):
    in_specs = (
        P(("table", "image"), None),
        P(("table", "image"), None),
        P(("table", "image")),
        P(("table", "image"), None),
        P(("table", "image"), None),
        P("image", None, "table"),
        P("image", None, "table"),
    )
    out_specs = P("image", "table")
    return jax.shard_map(
        per_device, mesh=mesh, in_specs=in_specs, out_specs=out_specs, check_vma=False
    )
```

profile of v0, /device:TPU:0, one launch (start us, length us, event | category | flops | bytes accessed | tf_op | source)
XLA Modules:
  0.0 23.2 jit_solution(13437901369900102544)
XLA Ops:
  0.0 21.9 %shard_map.73 = f32[1,512]{1,0:T(1,128)} custom-call(s32[4,16]{1,0:T(4,128)} %bitcast.8, s32[1,16]{1,0:T(1,128)} %bitcast.11, s32[4,16]{1,0:T(4,128)} %bitcast.9, bf16[4,16]{1,0:T(4,128)(2,1)} %bitcast.10, bf16[16,1920]{1,0:T(8,128)(2,1)} %traces_ref.1, f32[16,512]{1,0:T(8,128)} %bitcast.6, f32[16,512]{1,0:T(8,128)} %bitcast.7), custom_call_target="tpu_custom_call" | custom-call | flops 100000000 | bytes 1000000 | tf_op jit(solution)/shard_map/pallas_call | solution.py:330
  21.9 1.3 %copy.9 = f32[1,512]{1,0:T(1,128)} copy(f32[1,512]{1,0:T(1,128)} %shard_map.73) | data formatting | bytes 4096
where the time goes:
time: 23.4 us; the launch traced here: 23.2 us
  Pallas kernels  21.9 us (94%)
  local copies, waits for them, and re-layouts  1.26 us (5%)
    pallas_call x1, Pallas kernels, per_device(): pl.pallas_call(functools.partial(kernel, sizes, groups, half, scale), out...  21.9 us
    unnamed x1, local copies, waits for them, and re-layouts  1.26 us

commit v1 on v0

v1 whole, which is shorter than its diff:
```python
import functools
import math

import jax
import jax.numpy as jnp
from jax import lax
from jax.experimental import pallas as pl
from jax.experimental.pallas import tpu as pltpu
from jax.sharding import PartitionSpec as P

LANES = 128
FILTERS = 4
MESH = pl.DeviceIdType.MESH


def split_axis(count):
    if count == 16:
        return (4, 2, 2)
    root = math.isqrt(count)
    if root * root == count:
        return (root, root, 1)
    return (count, 1, 1)


def peers(size, at):
    found = []
    for step in range(1, size):
        if size & (size - 1):
            found.append(lax.rem(at + step, size))
            continue
        to, bit = at, 1
        while bit <= step:
            if step & bit:
                to = to + bit * (1 - 2 * lax.rem(to // bit, 2))
            bit *= 2
        found.append(to)
    return found


def eye_column(row, count):
    across = lax.broadcasted_iota(jnp.int32, (count, count), 1)
    down = lax.broadcasted_iota(jnp.int32, (count, count), 0)
    return jnp.sum(jnp.where(across == down, row, 0.0), axis=1, keepdims=True)


def selection(aperture, bucket, node, gain, nodes, half):
    count = aperture.shape[1]
    lane = lax.broadcasted_iota(jnp.int32, (count, 2 * half), 1)
    low = lane < half
    tile = jnp.where(low, lane, lane - half).astype(jnp.float32)
    offset = eye_column(bucket.astype(jnp.float32) * nodes, count)
    total = jnp.zeros((count, 2 * half), jnp.float32)
    for a in range(aperture.shape[0]):
        named = eye_column(aperture[a : a + 1].astype(jnp.float32), count)
        row = eye_column(node[a : a + 1].astype(jnp.float32), count) + offset
        weight = eye_column(gain[a : a + 1].astype(jnp.float32), count)
        total = total + jnp.where(named == tile, jnp.where(low, weight, row), 0.0)
    return total


def stack_of(added, nodes):
    count, samples = added.shape
    width = samples + LANES
    padded = jnp.concatenate([added, jnp.zeros((count, LANES), jnp.float32)], axis=1)
    first, second, third, fourth = (
        padded[b * nodes : (b + 1) * nodes] * (1.0 / (2 + 2 * b) ** 2) for b in range(FILTERS)
    )

    def both(values, lag):
        return pltpu.roll(values, lag, 1) + pltpu.roll(values, width - lag, 1)

    inner = (third + 2.0 * fourth) + both(fourth, 2)
    inner = (second + 2.0 * third) + both(inner, 2)
    inner = (first + 2.0 * second + third) + both(inner, 2)
    stack = 2.0 * inner + both(inner, 1)
    upper = pltpu.roll(stack, width - 1, 1)
    return stack[:, :samples], upper[:, :samples]


def partial_image(stack, upper, travel, spread):
    floor_value = jnp.floor(travel)
    fraction = travel - floor_value
    lower = floor_value.astype(jnp.int32)
    chunk = lax.shift_right_logical(lower, 7)
    inner = jnp.bitwise_and(lower, LANES - 1)
    pieces = []
    for c in range(travel.shape[1] // LANES):
        cells = slice(c * LANES, (c + 1) * LANES)
        here, within = chunk[:, cells], inner[:, cells]
        low = jnp.zeros(here.shape, jnp.float32)
        high = jnp.zeros(here.shape, jnp.float32)
        for k in range(stack.shape[1] // LANES):
            samples = slice(k * LANES, (k + 1) * LANES)
            mine = here == k
            picked = jnp.take_along_axis(stack[:, samples], within, axis=1, mode="promise_in_bounds")
            above = jnp.take_along_axis(upper[:, samples], within, axis=1, mode="promise_in_bounds")
            low = jnp.where(mine, picked, low)
            high = jnp.where(mine, above, high)
        part = fraction[:, cells]
        value = spread[:, cells] * ((1.0 - part) * low + part * high)
        pieces.append(jnp.sum(value, axis=0, keepdims=True))
    return jnp.concatenate(pieces, axis=1)


def kernel(
    sizes, groups, half, scale,
    aperture_hbm, bucket_hbm, node_hbm, gain_hbm, traces_ref, travel_ref, spread_ref,
    out_ref,
    aperture_ref, bucket_ref, node_ref, gain_ref,
    blocks, travels, spreads, parts, outgoing,
    load_sem, send_sem, recv_sem, table_send, table_recv, part_send, part_recv,
):
    size_z, size_y, size_c = sizes
    me = lax.axis_index("image")
    group = lax.axis_index("table")
    z = me // (size_y * size_c)
    y = lax.rem(me // size_c, size_y)
    core = lax.rem(me, size_c)
    count, samples = traces_ref.shape
    nodes = travel_ref.shape[0]
    rows = FILTERS * nodes

    def index(at_z, at_y, at_c):
        return (at_z * size_y + at_y) * size_c + at_c

    def slot_of(at_g, at_y, at_c):
        return (at_g * size_y + at_y) * size_c + at_c

    home = slot_of(group, y, core)
    loads = [
        pltpu.make_async_copy(source, landing, load_sem.at[k])
        for k, (source, landing) in enumerate((
            (aperture_hbm, aperture_ref), (bucket_hbm, bucket_ref), (node_hbm, node_ref), (gain_hbm, gain_ref),
            (traces_ref, blocks.at[home, :, pl.ds(0, samples)]),
            (travel_ref, travels.at[z]), (spread_ref, spreads.at[z]),
        ))
    ]
    for load in loads:
        load.start()

    line_z, line_y, line_c = peers(size_z, z), peers(size_y, y), peers(size_c, core)
    line_z = line_z[::-1]
    line_g = peers(groups, group)
    across = [(to_g, to_y) for to_g in line_g for to_y in line_y]
    across += [(to_g, y) for to_g in line_g] + [(group, to_y) for to_y in line_y]

    barrier = pltpu.get_barrier_semaphore()
    partners = [(to_g, index(z, to_y, core)) for to_g, to_y in across]
    partners += [(group, index(z, y, to)) for to in line_c]
    partners += [(group, index(to, y, core)) for to in line_z]
    for partner in partners:
        pl.semaphore_signal(barrier, inc=1, device_id=partner, device_id_type=MESH)

    with jax.named_scope("selection"):
        for load in loads[:4]:
            load.wait()
        blocks[home, :, samples:] = selection(
            aperture_ref[...], bucket_ref[...], node_ref[...], gain_ref[...], nodes, half
        ).astype(jnp.bfloat16)
        lane = lax.broadcasted_iota(jnp.int32, (rows, 2 * half), 1)
        tiles = [index(to, y, core) for to in (*line_z, z)]
        pick_weight = jnp.concatenate([jnp.where(lane == tile, 1.0, 0.0) for tile in tiles], axis=0).astype(jnp.bfloat16)
        pick_row = jnp.concatenate([jnp.where(lane == tile + half, 1.0, 0.0) for tile in tiles], axis=0).astype(jnp.bfloat16)
        loads[4].wait()

    with jax.named_scope("entry_barrier"):
        pl.semaphore_wait(barrier, len(partners))

    started = []

    def block_copy(slot, number, to):
        return pltpu.make_async_remote_copy(
            src_ref=blocks.at[slot],
            dst_ref=blocks.at[slot],
            send_sem=send_sem.at[number],
            recv_sem=recv_sem.at[slot],
            device_id=to,
            device_id_type=MESH,
        )

    def send(slot, to):
        copy = block_copy(slot, len(started), to)
        copy.start()
        started.append(copy)

    def receive(slot):
        block_copy(slot, 0, partners[0]).wait_recv()

    def send_core(slot):
        for to in line_c:
            send(slot, (group, index(z, y, to)))

    for to_g, to_y in across:
        send(home, (to_g, index(z, to_y, core)))
    send_core(home)
    table_copies = []
    for k, to in enumerate(line_z):
        for which, (source, landing) in enumerate(((travel_ref, travels), (spread_ref, spreads))):
            copy = pltpu.make_async_remote_copy(
                src_ref=source,
                dst_ref=landing.at[z],
                send_sem=table_send.at[which, k],
                recv_sem=table_recv.at[which, z],
                device_id=(group, index(to, y, core)),
                device_id_type=MESH,
            )
            copy.start()
            table_copies.append(copy)

    for at_g, at_y in across[::-1]:
        slot = slot_of(at_g, at_y, core)
        receive(slot)
        send_core(slot)
    for at_c in line_c:
        receive(slot_of(group, y, at_c))
    for at_g, at_y in across[::-1]:
        for at_c in line_c:
            receive(slot_of(at_g, at_y, at_c))

    total = groups * size_y * size_c * count
    with jax.named_scope("stack"):
        chosen = blocks[:, :, samples:].reshape(total, 2 * half)
        dims = (((1,), (1,)), ((), ()))
        weight = lax.dot_general(pick_weight, chosen, dims, preferred_element_type=jnp.float32)
        row = lax.dot_general(pick_row, chosen, dims, preferred_element_type=jnp.float32)
        wanted = lax.broadcasted_iota(jnp.int32, (rows, total), 0).astype(jnp.float32)
        data = blocks[:, :, :samples].reshape(total, samples)
        stacks = []
        for k in range(size_z):
            mine = slice(k * rows, (k + 1) * rows)
            member = jnp.where(row[mine] == wanted, weight[mine], 0.0).astype(jnp.bfloat16)
            stacks.append(jnp.dot(member, data, preferred_element_type=jnp.float32))

    part_copies = []
    with jax.named_scope("other_images"):
        for k, to in enumerate(line_z):
            stack, upper = stack_of(stacks[k], nodes)
            for which, landing in enumerate((travels, spreads)):
                pltpu.make_async_remote_copy(
                    src_ref=landing.at[to],
                    dst_ref=landing.at[to],
                    send_sem=table_send.at[which, k],
                    recv_sem=table_recv.at[which, to],
                    device_id=(group, index(to, y, core)),
                    device_id_type=MESH,
                ).wait_recv()
            outgoing[k] = partial_image(stack, upper, travels[to], spreads[to])
            copy = pltpu.make_async_remote_copy(
                src_ref=outgoing.at[k],
                dst_ref=parts.at[z],
                send_sem=part_send.at[k],
                recv_sem=part_recv.at[z],
                device_id=(group, index(to, y, core)),
                device_id_type=MESH,
            )
            copy.start()
            part_copies.append(copy)
    with jax.named_scope("own_image"):
        for load in loads[5:]:
            load.wait()
        stack, upper = stack_of(stacks[size_z - 1], nodes)
        image = partial_image(stack, upper, travels[z], spreads[z])
    with jax.named_scope("last_waits"):
        for copy in started:
            copy.wait_send()
        for copy in table_copies:
            copy.wait_send()
        for k, to in enumerate(line_z):
            pltpu.make_async_remote_copy(
                src_ref=outgoing.at[k],
                dst_ref=parts.at[to],
                send_sem=part_send.at[k],
                recv_sem=part_recv.at[to],
                device_id=(group, index(to, y, core)),
                device_id_type=MESH,
            ).wait_recv()
            image = image + parts[to]
        for copy in part_copies:
            copy.wait_send()
    out_ref[...] = image * scale


def per_device(traces, aperture, bucket, table_node, entry_gain, travel, spread):
    tiles = lax.axis_size("image")
    groups = lax.axis_size("table")
    count, samples = traces.shape
    nodes, cells = travel.shape[1], travel.shape[2]
    half = -(-tiles // (LANES // 2)) * (LANES // 2)
    sizes = split_axis(tiles)
    size_z, size_y = sizes[:2]
    plane = size_y * sizes[2]
    scale = 1.0 / math.sqrt(count * groups * aperture.shape[1])
    vmem = pl.BlockSpec(memory_space=pltpu.VMEM)
    whole = pl.BlockSpec(memory_space=pl.ANY)
    return pl.pallas_call(
        functools.partial(kernel, sizes, groups, half, scale),
        out_shape=jax.ShapeDtypeStruct((1, cells), jnp.float32),
        in_specs=[whole] * 7,
        out_specs=vmem,
        scratch_shapes=[
            pltpu.VMEM(aperture.shape[::-1], jnp.int32),
            pltpu.VMEM((1, count), jnp.int32),
            pltpu.VMEM(table_node.shape[::-1], jnp.int32),
            pltpu.VMEM(entry_gain.shape[::-1], jnp.bfloat16),
            pltpu.VMEM((groups * plane, count, samples + 2 * half), jnp.bfloat16),
            pltpu.VMEM((size_z, nodes, cells), jnp.float32),
            pltpu.VMEM((size_z, nodes, cells), jnp.float32),
            pltpu.VMEM((size_z, 1, cells), jnp.float32),
            pltpu.VMEM((max(size_z - 1, 1), 1, cells), jnp.float32),
            pltpu.SemaphoreType.DMA((7,)),
            pltpu.SemaphoreType.DMA((groups * plane,)),
            pltpu.SemaphoreType.DMA((groups * plane,)),
            pltpu.SemaphoreType.DMA((2, max(size_z - 1, 1))),
            pltpu.SemaphoreType.DMA((2, size_z)),
            pltpu.SemaphoreType.DMA((max(size_z - 1, 1),)),
            pltpu.SemaphoreType.DMA((size_z,)),
        ],
        compiler_params=pltpu.CompilerParams(
            collective_id=0, has_side_effects=True, vmem_limit_bytes=56 * 1024 * 1024
        ),
        cost_estimate=pl.CostEstimate(flops=10**8, bytes_accessed=10**6, transcendentals=0),
    )(aperture.T, bucket.reshape(1, count), table_node.T, entry_gain.T, traces, travel[0], spread[0])


def solution(mesh):
    in_specs = (
        P(("table", "image"), None),
        P(("table", "image"), None),
        P(("table", "image")),
        P(("table", "image"), None),
        P(("table", "image"), None),
        P("image", None, "table"),
        P("image", None, "table"),
    )
    out_specs = P("image", "table")
    return jax.shard_map(
        per_device, mesh=mesh, in_specs=in_specs, out_specs=out_specs, check_vma=False
    )
```

time: 23.4 us -> 19.1 us (0.82)
  Pallas kernels: 21.9 us -> 17.7 us
    pallas_call x1, Pallas kernels: 21.9 us -> 17.7 us  [per_device(): pl.pallas_call(functools.partial(kernel, sizes, groups, half, scale), out...]
where the time goes in v1:
time: 19.1 us; the launch traced here: 19 us
  Pallas kernels  17.7 us (93%)
  local copies, waits for them, and re-layouts  1.26 us (7%)
    pallas_call x1, Pallas kernels, per_device(): pl.pallas_call(functools.partial(kernel, sizes, groups, half, scale), out...  17.7 us
    unnamed x1, local copies, waits for them, and re-layouts  1.26 us

profile of v1, /device:TPU:0, one launch (start us, length us, event | category | flops | bytes accessed | tf_op | source)
XLA Modules:
  0.0 19.0 jit_solution(480087215294919630)
XLA Ops:
  0.0 17.7 %shard_map.73 = f32[1,512]{1,0:T(1,128)} custom-call(s32[4,16]{1,0:T(4,128)} %bitcast.8, s32[1,16]{1,0:T(1,128)} %bitcast.11, s32[4,16]{1,0:T(4,128)} %bitcast.9, bf16[4,16]{1,0:T(4,128)(2,1)} %bitcast.10, bf16[16,1920]{1,0:T(8,128)(2,1)} %traces_ref.1, f32[16,512]{1,0:T(8,128)} %bitcast.6, f32[16,512]{1,0:T(8,128)} %bitcast.7), custom_call_target="tpu_custom_call" | custom-call | flops 100000000 | bytes 1000000 | tf_op jit(solution)/shard_map/pallas_call | solution.py:295
  17.7 1.3 %copy.9 = f32[1,512]{1,0:T(1,128)} copy(f32[1,512]{1,0:T(1,128)} %shard_map.73) | data formatting | bytes 4096

commit v2 on v1

--- a/solution.py
+++ b/solution.py
@@ -316,10 +316,12 @@
             pltpu.SemaphoreType.DMA((size_z,)),
         ],
         compiler_params=pltpu.CompilerParams(
-            collective_id=0, has_side_effects=True, vmem_limit_bytes=56 * 1024 * 1024
+            collective_id=0, has_side_effects=True, vmem_limit_bytes=24 * 1024 * 1024
         ),
         cost_estimate=pl.CostEstimate(flops=10**8, bytes_accessed=10**6, transcendentals=0),
-    )(aperture.T, bucket.reshape(1, count), table_node.T, entry_gain.T, traces, travel[0], spread[0])
+    )(*(pltpu.with_memory_space_constraint(operand, pltpu.HBM) for operand in (
+        aperture.T, bucket.reshape(1, count), table_node.T, entry_gain.T, traces, travel[0], spread[0]
+    )))
 
 
 def solution(mesh):

time: 19.1 us -> 17.8 us (0.932)
  local copies, waits for them, and re-layouts: 1.26 us -> 0.58 us
  Pallas kernels: 17.7 us -> 17.1 us
    unnamed x1, local copies, waits for them, and re-layouts: 1.26 us -> 0.58 us
    pallas_call x1, Pallas kernels: 17.7 us -> 17.1 us  [per_device(): pl.pallas_call(functools.partial(kernel, sizes, groups, half, scale), out...]
where the time goes in v2:
time: 17.8 us; the launch traced here: 17.7 us
  Pallas kernels  17.1 us (96%)
  local copies, waits for them, and re-layouts  0.58 us (3%)
    pallas_call x1, Pallas kernels, per_device(): pl.pallas_call(functools.partial(kernel, sizes, groups, half, scale), out...  17.1 us
    unnamed x1, local copies, waits for them, and re-layouts  0.58 us

profile of v2, /device:TPU:0, one launch (start us, length us, event | category | flops | bytes accessed | tf_op | source)
XLA Modules:
  0.0 17.7 jit_solution(11159903546074046073)
XLA Ops:
  0.0 17.1 %shard_map.73 = f32[1,512]{1,0:T(1,128)S(1)} custom-call(s32[4,16]{1,0:T(4,128)} %bitcast.8, s32[1,16]{1,0:T(1,128)} %bitcast.11, s32[4,16]{1,0:T(4,128)} %bitcast.9, bf16[4,16]{1,0:T(4,128)(2,1)} %bitcast.10, bf16[16,1920]{1,0:T(8,128)(2,1)} %traces_ref.1, f32[16,512]{1,0:T(8,128)} %bitcast.6, f32[16,512]{1,0:T(8,128)} %bitcast.7), custom_call_target="tpu_custom_call" | custom-call | flops 100000000 | bytes 1000000 | tf_op jit(solution)/shard_map/pallas_call | solution.py:295
  17.1 0.6 %copy.9 = f32[1,512]{1,0:T(1,128)} copy(f32[1,512]{1,0:T(1,128)S(1)} %shard_map.73) | data formatting | bytes 4096

commit v3 on v2

--- a/solution.py
+++ b/solution.py
@@ -139,7 +139,8 @@
         load.start()
 
     line_z, line_y, line_c = peers(size_z, z), peers(size_y, y), peers(size_c, core)
-    line_z = line_z[::-1]
+    if size_z == 4:
+        line_z = [line_z[0], line_z[2], line_z[1]]
     line_g = peers(groups, group)
     across = [(to_g, to_y) for to_g in line_g for to_y in line_y]
     across += [(to_g, y) for to_g in line_g] + [(group, to_y) for to_y in line_y]
@@ -231,10 +232,11 @@
             member = jnp.where(row[mine] == wanted, weight[mine], 0.0).astype(jnp.bfloat16)
             stacks.append(jnp.dot(member, data, preferred_element_type=jnp.float32))
 
+    filtered = [stack_of(stacks[k], nodes) for k in range(size_z - 1)]
     part_copies = []
     with jax.named_scope("other_images"):
         for k, to in enumerate(line_z):
-            stack, upper = stack_of(stacks[k], nodes)
+            stack, upper = filtered[k]
             for which, landing in enumerate((travels, spreads)):
                 pltpu.make_async_remote_copy(
                     src_ref=landing.at[to],

time: 17.8 us -> 16.7 us (0.938); the launches traced: 17.7 us -> 16.4 us
  Pallas kernels: 17.1 us -> 15.8 us
    pallas_call x1, Pallas kernels: 17.1 us -> 15.8 us  [per_device(): pl.pallas_call(functools.partial(kernel, sizes, groups, half, scale), out...]
where the time goes in v3:
time: 16.7 us; the launch traced here: 16.4 us
  Pallas kernels  15.8 us (95%)
  local copies, waits for them, and re-layouts  0.58 us (3%)
    pallas_call x1, Pallas kernels, per_device(): pl.pallas_call(functools.partial(kernel, sizes, groups, half, scale), out...  15.8 us
    unnamed x1, local copies, waits for them, and re-layouts  0.58 us

profile of v3, /device:TPU:0, one launch (start us, length us, event | category | flops | bytes accessed | tf_op | source)
XLA Modules:
  0.0 16.4 jit_solution(8146505119282645008)
XLA Ops:
  0.0 15.8 %shard_map.73 = f32[1,512]{1,0:T(1,128)S(1)} custom-call(s32[4,16]{1,0:T(4,128)} %bitcast.8, s32[1,16]{1,0:T(1,128)} %bitcast.11, s32[4,16]{1,0:T(4,128)} %bitcast.9, bf16[4,16]{1,0:T(4,128)(2,1)} %bitcast.10, bf16[16,1920]{1,0:T(8,128)(2,1)} %traces_ref.1, f32[16,512]{1,0:T(8,128)} %bitcast.6, f32[16,512]{1,0:T(8,128)} %bitcast.7), custom_call_target="tpu_custom_call" | custom-call | flops 100000000 | bytes 1000000 | tf_op jit(solution)/shard_map/pallas_call | solution.py:297
  15.8 0.6 %copy.9 = f32[1,512]{1,0:T(1,128)} copy(f32[1,512]{1,0:T(1,128)S(1)} %shard_map.73) | data formatting | bytes 4096

commit v4 on v3

--- a/solution.py
+++ b/solution.py
@@ -9,6 +9,10 @@
 from jax.sharding import PartitionSpec as P
 
 LANES = 128
+IMAGES = ((1, 3, 2), (0, 2, 3), (0, 3, 1), (0, 2, 1))
+TABLES = ((1, 3, 2), (0, 2, 3), (0, 3, 1), (0, 2, 1))
+LEVELS = 32000.0
+FACTORS = ((1,), (2, 1), (1, 2, 1), (0, 0, 2, 1))
 FILTERS = 4
 MESH = pl.DeviceIdType.MESH
 
@@ -37,44 +41,52 @@
     return found
 
 
+def choose(at, values):
+    found = jnp.int32(values[0])
+    for k, value in enumerate(values[1:], 1):
+        found = jnp.where(at == k, value, found)
+    return found
+
+
 def eye_column(row, count):
     across = lax.broadcasted_iota(jnp.int32, (count, count), 1)
     down = lax.broadcasted_iota(jnp.int32, (count, count), 0)
     return jnp.sum(jnp.where(across == down, row, 0.0), axis=1, keepdims=True)
 
 
-def selection(aperture, bucket, node, gain, nodes, half):
+def selection(aperture, node, gain, unit, half):
     count = aperture.shape[1]
     lane = lax.broadcasted_iota(jnp.int32, (count, 2 * half), 1)
     low = lane < half
     tile = jnp.where(low, lane, lane - half).astype(jnp.float32)
-    offset = eye_column(bucket.astype(jnp.float32) * nodes, count)
     total = jnp.zeros((count, 2 * half), jnp.float32)
     for a in range(aperture.shape[0]):
         named = eye_column(aperture[a : a + 1].astype(jnp.float32), count)
-        row = eye_column(node[a : a + 1].astype(jnp.float32), count) + offset
-        weight = eye_column(gain[a : a + 1].astype(jnp.float32), count)
+        row = eye_column(node[a : a + 1].astype(jnp.float32), count)
+        weight = eye_column(gain[a : a + 1].astype(jnp.float32), count) * unit
         total = total + jnp.where(named == tile, jnp.where(low, weight, row), 0.0)
     return total
 
 
-def stack_of(added, nodes):
-    count, samples = added.shape
+def antialias(traces, bucket):
+    count, samples = traces.shape
     width = samples + LANES
-    padded = jnp.concatenate([added, jnp.zeros((count, LANES), jnp.float32)], axis=1)
-    first, second, third, fourth = (
-        padded[b * nodes : (b + 1) * nodes] * (1.0 / (2 + 2 * b) ** 2) for b in range(FILTERS)
-    )
+    padded = jnp.concatenate([traces, jnp.zeros((count, LANES), jnp.float32)], axis=1)
+    factors = []
+    for power in range(FILTERS):
+        factor = jnp.zeros(bucket.shape, jnp.float32)
+        for b, terms in enumerate(FACTORS):
+            if power < len(terms) and terms[power]:
+                factor = jnp.where(bucket == b, terms[power] / (2 + 2 * b) ** 2, factor)
+        factors.append(factor)
 
     def both(values, lag):
         return pltpu.roll(values, lag, 1) + pltpu.roll(values, width - lag, 1)
 
-    inner = (third + 2.0 * fourth) + both(fourth, 2)
-    inner = (second + 2.0 * third) + both(inner, 2)
-    inner = (first + 2.0 * second + third) + both(inner, 2)
-    stack = 2.0 * inner + both(inner, 1)
-    upper = pltpu.roll(stack, width - 1, 1)
-    return stack[:, :samples], upper[:, :samples]
+    inner = factors[3] * padded
+    for power in (2, 1, 0):
+        inner = factors[power] * padded + both(inner, 2)
+    return (2.0 * inner + both(inner, 1))[:, :samples]
 
 
 def partial_image(stack, upper, travel, spread):
@@ -107,7 +119,7 @@
     aperture_hbm, bucket_hbm, node_hbm, gain_hbm, traces_ref, travel_ref, spread_ref,
     out_ref,
     aperture_ref, bucket_ref, node_ref, gain_ref,
-    blocks, travels, spreads, parts, outgoing,
+    traces, blocks, picks, halves, travels, spread_own, spreads, parts, outgoing,
     load_sem, send_sem, recv_sem, table_send, table_recv, part_send, part_recv,
 ):
     size_z, size_y, size_c = sizes
@@ -118,7 +130,7 @@
     core = lax.rem(me, size_c)
     count, samples = traces_ref.shape
     nodes = travel_ref.shape[0]
-    rows = FILTERS * nodes
+    rows = nodes
 
     def index(at_z, at_y, at_c):
         return (at_z * size_y + at_y) * size_c + at_c
@@ -127,20 +139,11 @@
         return (at_g * size_y + at_y) * size_c + at_c
 
     home = slot_of(group, y, core)
-    loads = [
-        pltpu.make_async_copy(source, landing, load_sem.at[k])
-        for k, (source, landing) in enumerate((
-            (aperture_hbm, aperture_ref), (bucket_hbm, bucket_ref), (node_hbm, node_ref), (gain_hbm, gain_ref),
-            (traces_ref, blocks.at[home, :, pl.ds(0, samples)]),
-            (travel_ref, travels.at[z]), (spread_ref, spreads.at[z]),
-        ))
-    ]
-    for load in loads:
-        load.start()
-
     line_z, line_y, line_c = peers(size_z, z), peers(size_y, y), peers(size_c, core)
+    send_z = line_z
     if size_z == 4:
-        line_z = [line_z[0], line_z[2], line_z[1]]
+        line_z = [choose(z, [row[k] for row in IMAGES]) for k in range(3)]
+        send_z = [choose(z, [row[k] for row in TABLES]) for k in range(3)]
     line_g = peers(groups, group)
     across = [(to_g, to_y) for to_g in line_g for to_y in line_y]
     across += [(to_g, y) for to_g in line_g] + [(group, to_y) for to_y in line_y]
@@ -152,40 +155,69 @@
     for partner in partners:
         pl.semaphore_signal(barrier, inc=1, device_id=partner, device_id_type=MESH)
 
+    loads = [
+        pltpu.make_async_copy(source, landing, load_sem.at[k])
+        for k, (source, landing) in enumerate((
+            (aperture_hbm, aperture_ref), (bucket_hbm, bucket_ref), (node_hbm, node_ref), (gain_hbm, gain_ref),
+            (traces_ref, traces),
+            (travel_ref, travels.at[z]), (spread_ref, spread_own),
+        ))
+    ]
+    for load in loads:
+        load.start()
+
     with jax.named_scope("selection"):
-        for load in loads[:4]:
+        for load in loads[:5]:
             load.wait()
-        blocks[home, :, samples:] = selection(
-            aperture_ref[...], bucket_ref[...], node_ref[...], gain_ref[...], nodes, half
-        ).astype(jnp.bfloat16)
+        bucket = eye_column(bucket_ref[...].astype(jnp.float32), count)
+        smooth = antialias(traces[...].astype(jnp.float32), bucket)
+        largest = jnp.maximum(jnp.max(jnp.abs(smooth), axis=1, keepdims=True), 1e-30)
+        unit = jnp.exp2(jnp.ceil(jnp.log2(largest))).astype(jnp.bfloat16).astype(jnp.float32)
+        levels = jnp.round(smooth * (LEVELS / unit))
+        blocks[home] = levels.astype(jnp.int32).astype(jnp.int16)
+        picks[home] = selection(aperture_ref[...], node_ref[...], gain_ref[...], unit, half).astype(jnp.bfloat16)
         lane = lax.broadcasted_iota(jnp.int32, (rows, 2 * half), 1)
         tiles = [index(to, y, core) for to in (*line_z, z)]
         pick_weight = jnp.concatenate([jnp.where(lane == tile, 1.0, 0.0) for tile in tiles], axis=0).astype(jnp.bfloat16)
         pick_row = jnp.concatenate([jnp.where(lane == tile + half, 1.0, 0.0) for tile in tiles], axis=0).astype(jnp.bfloat16)
-        loads[4].wait()
+        loads[6].wait()
+        spreads[z] = (spread_own[...] * LEVELS + 0.5).astype(jnp.int32).astype(jnp.int16)
 
     with jax.named_scope("entry_barrier"):
         pl.semaphore_wait(barrier, len(partners))
 
     started = []
 
-    def block_copy(slot, number, to):
-        return pltpu.make_async_remote_copy(
-            src_ref=blocks.at[slot],
-            dst_ref=blocks.at[slot],
-            send_sem=send_sem.at[number],
-            recv_sem=recv_sem.at[slot],
-            device_id=to,
-            device_id_type=MESH,
-        )
+    def block_copies(slot, number, to):
+        return [
+            pltpu.make_async_remote_copy(
+                src_ref=landing.at[slot],
+                dst_ref=landing.at[slot],
+                send_sem=send_sem.at[which, number],
+                recv_sem=recv_sem.at[which, slot],
+                device_id=to,
+                device_id_type=MESH,
+            )
+            for which, landing in enumerate((picks, blocks))
+        ]
 
     def send(slot, to):
-        copy = block_copy(slot, len(started), to)
-        copy.start()
-        started.append(copy)
+        copies = block_copies(slot, len(started) // 2, to)
+        for copy in copies:
+            copy.start()
+        started.extend(copies)
 
     def receive(slot):
-        block_copy(slot, 0, partners[0]).wait_recv()
+        for copy in block_copies(slot, 0, partners[0]):
+            copy.wait_recv()
+
+    places = groups * size_y * size_c
+
+    def split(slot):
+        whole = blocks[slot].astype(jnp.int32).astype(jnp.float32)
+        upper = whole.astype(jnp.bfloat16)
+        halves[slot] = upper
+        halves[places + slot] = (whole - upper.astype(jnp.float32)).astype(jnp.bfloat16)
 
     def send_core(slot):
         for to in line_c:
@@ -195,8 +227,8 @@
         send(home, (to_g, index(z, to_y, core)))
     send_core(home)
     table_copies = []
-    for k, to in enumerate(line_z):
-        for which, (source, landing) in enumerate(((travel_ref, travels), (spread_ref, spreads))):
+    for k, to in enumerate(send_z):
+        for which, (source, landing) in enumerate(((travel_ref, travels), (spreads.at[z], spreads))):
             copy = pltpu.make_async_remote_copy(
                 src_ref=source,
                 dst_ref=landing.at[z],
@@ -208,35 +240,37 @@
             copy.start()
             table_copies.append(copy)
 
+    split(home)
     for at_g, at_y in across[::-1]:
         slot = slot_of(at_g, at_y, core)
         receive(slot)
         send_core(slot)
+        split(slot)
     for at_c in line_c:
         receive(slot_of(group, y, at_c))
+        split(slot_of(group, y, at_c))
     for at_g, at_y in across[::-1]:
         for at_c in line_c:
             receive(slot_of(at_g, at_y, at_c))
-
-    total = groups * size_y * size_c * count
+            split(slot_of(at_g, at_y, at_c))
+
+    total = places * count
     with jax.named_scope("stack"):
-        chosen = blocks[:, :, samples:].reshape(total, 2 * half)
+        chosen = picks[...].reshape(total, 2 * half)
         dims = (((1,), (1,)), ((), ()))
         weight = lax.dot_general(pick_weight, chosen, dims, preferred_element_type=jnp.float32)
         row = lax.dot_general(pick_row, chosen, dims, preferred_element_type=jnp.float32)
-        wanted = lax.broadcasted_iota(jnp.int32, (rows, total), 0).astype(jnp.float32)
-        data = blocks[:, :, :samples].reshape(total, samples)
-        stacks = []
-        for k in range(size_z):
-            mine = slice(k * rows, (k + 1) * rows)
-            member = jnp.where(row[mine] == wanted, weight[mine], 0.0).astype(jnp.bfloat16)
-            stacks.append(jnp.dot(member, data, preferred_element_type=jnp.float32))
-
-    filtered = [stack_of(stacks[k], nodes) for k in range(size_z - 1)]
+        wanted = lax.rem(lax.broadcasted_iota(jnp.int32, row.shape, 0), rows).astype(jnp.float32)
+        member = jnp.where(row == wanted, weight, 0.0).astype(jnp.bfloat16)
+        member = jnp.concatenate([member, member], axis=1)
+        data = halves[...].reshape(2 * total, samples)
+        stacks = jnp.dot(member, data, preferred_element_type=jnp.float32)
+        uppers = pltpu.roll(stacks, samples - 1, 1)
+
     part_copies = []
     with jax.named_scope("other_images"):
         for k, to in enumerate(line_z):
-            stack, upper = filtered[k]
+            mine = slice(k * rows, (k + 1) * rows)
             for which, landing in enumerate((travels, spreads)):
                 pltpu.make_async_remote_copy(
                     src_ref=landing.at[to],
@@ -246,7 +280,8 @@
                     device_id=(group, index(to, y, core)),
                     device_id_type=MESH,
                 ).wait_recv()
-            outgoing[k] = partial_image(stack, upper, travels[to], spreads[to])
+            other = spreads[to].astype(jnp.int32).astype(jnp.float32)
+            outgoing[k] = partial_image(stacks[mine], uppers[mine], travels[to], other) * (1.0 / LEVELS)
             copy = pltpu.make_async_remote_copy(
                 src_ref=outgoing.at[k],
                 dst_ref=parts.at[z],
@@ -258,10 +293,9 @@
             copy.start()
             part_copies.append(copy)
     with jax.named_scope("own_image"):
-        for load in loads[5:]:
-            load.wait()
-        stack, upper = stack_of(stacks[size_z - 1], nodes)
-        image = partial_image(stack, upper, travels[z], spreads[z])
+        loads[5].wait()
+        mine = slice((size_z - 1) * rows, size_z * rows)
+        image = partial_image(stacks[mine], uppers[mine], travels[z], spread_own[...])
     with jax.named_scope("last_waits"):
         for copy in started:
             copy.wait_send()
@@ -279,7 +313,7 @@
             image = image + parts[to]
         for copy in part_copies:
             copy.wait_send()
-    out_ref[...] = image * scale
+    out_ref[...] = image * (scale / LEVELS)
 
 
 def per_device(traces, aperture, bucket, table_node, entry_gain, travel, spread):
@@ -304,14 +338,18 @@
             pltpu.VMEM((1, count), jnp.int32),
             pltpu.VMEM(table_node.shape[::-1], jnp.int32),
             pltpu.VMEM(entry_gain.shape[::-1], jnp.bfloat16),
-            pltpu.VMEM((groups * plane, count, samples + 2 * half), jnp.bfloat16),
+            pltpu.VMEM(traces.shape, jnp.bfloat16),
+            pltpu.VMEM((groups * plane, count, samples), jnp.int16),
+            pltpu.VMEM((groups * plane, count, 2 * half), jnp.bfloat16),
+            pltpu.VMEM((2 * groups * plane, count, samples), jnp.bfloat16),
             pltpu.VMEM((size_z, nodes, cells), jnp.float32),
-            pltpu.VMEM((size_z, nodes, cells), jnp.float32),
+            pltpu.VMEM((nodes, cells), jnp.float32),
+            pltpu.VMEM((size_z, nodes, cells), jnp.int16),
             pltpu.VMEM((size_z, 1, cells), jnp.float32),
             pltpu.VMEM((max(size_z - 1, 1), 1, cells), jnp.float32),
             pltpu.SemaphoreType.DMA((7,)),
-            pltpu.SemaphoreType.DMA((groups * plane,)),
-            pltpu.SemaphoreType.DMA((groups * plane,)),
+            pltpu.SemaphoreType.DMA((2, groups * plane)),
+            pltpu.SemaphoreType.DMA((2, groups * plane)),
             pltpu.SemaphoreType.DMA((2, max(size_z - 1, 1))),
             pltpu.SemaphoreType.DMA((2, size_z)),
             pltpu.SemaphoreType.DMA((max(size_z - 1, 1),)),

time: 16.7 us -> 15.9 us (0.952)
  Pallas kernels: 15.8 us -> 15.1 us
    pallas_call x1, Pallas kernels: 15.8 us -> 15.1 us  [per_device(): pl.pallas_call(functools.partial(kernel, sizes, groups, half, scale), out...]
where the time goes in v4:
time: 15.9 us; the launch traced here: 15.7 us
  Pallas kernels  15.1 us (95%)
  local copies, waits for them, and re-layouts  0.58 us (4%)
    pallas_call x1, Pallas kernels, per_device(): pl.pallas_call(functools.partial(kernel, sizes, groups, half, scale), out...  15.1 us
    unnamed x1, local copies, waits for them, and re-layouts  0.58 us

profile of v4, /device:TPU:0, one launch (start us, length us, event | category | flops | bytes accessed | tf_op | source)
XLA Modules:
  0.0 15.7 jit_solution(3563261360511620088)
XLA Ops:
  0.0 15.1 %shard_map.73 = f32[1,512]{1,0:T(1,128)S(1)} custom-call(s32[4,16]{1,0:T(4,128)} %bitcast.8, s32[1,16]{1,0:T(1,128)} %bitcast.11, s32[4,16]{1,0:T(4,128)} %bitcast.9, bf16[4,16]{1,0:T(4,128)(2,1)} %bitcast.10, bf16[16,1920]{1,0:T(8,128)(2,1)} %traces_ref.1, f32[16,512]{1,0:T(8,128)} %bitcast.6, f32[16,512]{1,0:T(8,128)} %bitcast.7), custom_call_target="tpu_custom_call" | custom-call | flops 100000000 | bytes 1000000 | tf_op jit(solution)/shard_map/pallas_call | solution.py:331
  15.1 0.6 %copy.9 = f32[1,512]{1,0:T(1,128)} copy(f32[1,512]{1,0:T(1,128)S(1)} %shard_map.73) | data formatting | bytes 4096

commit v5 on v4

--- a/solution.py
+++ b/solution.py
@@ -10,7 +10,7 @@
 
 LANES = 128
 IMAGES = ((1, 3, 2), (0, 2, 3), (0, 3, 1), (0, 2, 1))
-TABLES = ((1, 3, 2), (0, 2, 3), (0, 3, 1), (0, 2, 1))
+TABLES = ((3, 2, 1), (0, 3, 2), (3, 0, 1), (2, 1, 0))
 LEVELS = 32000.0
 FACTORS = ((1,), (2, 1), (1, 2, 1), (0, 0, 2, 1))
 FILTERS = 4
@@ -54,7 +54,7 @@
     return jnp.sum(jnp.where(across == down, row, 0.0), axis=1, keepdims=True)
 
 
-def selection(aperture, node, gain, unit, half):
+def selection(aperture, node, gain, half):
     count = aperture.shape[1]
     lane = lax.broadcasted_iota(jnp.int32, (count, 2 * half), 1)
     low = lane < half
@@ -63,7 +63,7 @@
     for a in range(aperture.shape[0]):
         named = eye_column(aperture[a : a + 1].astype(jnp.float32), count)
         row = eye_column(node[a : a + 1].astype(jnp.float32), count)
-        weight = eye_column(gain[a : a + 1].astype(jnp.float32), count) * unit
+        weight = eye_column(gain[a : a + 1].astype(jnp.float32), count)
         total = total + jnp.where(named == tile, jnp.where(low, weight, row), 0.0)
     return total
 
@@ -89,7 +89,7 @@
     return (2.0 * inner + both(inner, 1))[:, :samples]
 
 
-def partial_image(stack, upper, travel, spread):
+def partial_image(stack, unit, travel, spread):
     floor_value = jnp.floor(travel)
     fraction = travel - floor_value
     lower = floor_value.astype(jnp.int32)
@@ -99,18 +99,18 @@
     for c in range(travel.shape[1] // LANES):
         cells = slice(c * LANES, (c + 1) * LANES)
         here, within = chunk[:, cells], inner[:, cells]
-        low = jnp.zeros(here.shape, jnp.float32)
-        high = jnp.zeros(here.shape, jnp.float32)
+        pair = jnp.zeros(here.shape, jnp.int32)
         for k in range(stack.shape[1] // LANES):
             samples = slice(k * LANES, (k + 1) * LANES)
             mine = here == k
             picked = jnp.take_along_axis(stack[:, samples], within, axis=1, mode="promise_in_bounds")
-            above = jnp.take_along_axis(upper[:, samples], within, axis=1, mode="promise_in_bounds")
-            low = jnp.where(mine, picked, low)
-            high = jnp.where(mine, above, high)
+            pair = jnp.where(mine, picked, pair)
+        high = lax.shift_right_arithmetic(pair, 16)
+        low = (pair - lax.shift_left(high, 16)).astype(jnp.float32) - 32768.0
+        high = high.astype(jnp.float32)
         part = fraction[:, cells]
         value = spread[:, cells] * ((1.0 - part) * low + part * high)
-        pieces.append(jnp.sum(value, axis=0, keepdims=True))
+        pieces.append(jnp.sum(value * unit, axis=0, keepdims=True))
     return jnp.concatenate(pieces, axis=1)
 
 
@@ -148,13 +148,6 @@
     across = [(to_g, to_y) for to_g in line_g for to_y in line_y]
     across += [(to_g, y) for to_g in line_g] + [(group, to_y) for to_y in line_y]
 
-    barrier = pltpu.get_barrier_semaphore()
-    partners = [(to_g, index(z, to_y, core)) for to_g, to_y in across]
-    partners += [(group, index(z, y, to)) for to in line_c]
-    partners += [(group, index(to, y, core)) for to in line_z]
-    for partner in partners:
-        pl.semaphore_signal(barrier, inc=1, device_id=partner, device_id_type=MESH)
-
     loads = [
         pltpu.make_async_copy(source, landing, load_sem.at[k])
         for k, (source, landing) in enumerate((
@@ -163,25 +156,29 @@
             (travel_ref, travels.at[z]), (spread_ref, spread_own),
         ))
     ]
-    for load in loads:
-        load.start()
+    for k in (0, 1, 2, 3, 4, 6, 5):
+        loads[k].start()
+
+    barrier = pltpu.get_barrier_semaphore()
+    partners = [(to_g, index(z, to_y, core)) for to_g, to_y in across]
+    partners += [(group, index(z, y, to)) for to in line_c]
+    partners += [(group, index(to, y, core)) for to in line_z]
+    for partner in partners:
+        pl.semaphore_signal(barrier, inc=1, device_id=partner, device_id_type=MESH)
 
     with jax.named_scope("selection"):
-        for load in loads[:5]:
+        for load in loads[:4]:
             load.wait()
         bucket = eye_column(bucket_ref[...].astype(jnp.float32), count)
+        chosen = selection(aperture_ref[...], node_ref[...], gain_ref[...], half)
+        lane = lax.broadcasted_iota(jnp.int32, chosen.shape, 1)
+        loads[4].wait()
         smooth = antialias(traces[...].astype(jnp.float32), bucket)
         largest = jnp.maximum(jnp.max(jnp.abs(smooth), axis=1, keepdims=True), 1e-30)
         unit = jnp.exp2(jnp.ceil(jnp.log2(largest))).astype(jnp.bfloat16).astype(jnp.float32)
         levels = jnp.round(smooth * (LEVELS / unit))
         blocks[home] = levels.astype(jnp.int32).astype(jnp.int16)
-        picks[home] = selection(aperture_ref[...], node_ref[...], gain_ref[...], unit, half).astype(jnp.bfloat16)
-        lane = lax.broadcasted_iota(jnp.int32, (rows, 2 * half), 1)
-        tiles = [index(to, y, core) for to in (*line_z, z)]
-        pick_weight = jnp.concatenate([jnp.where(lane == tile, 1.0, 0.0) for tile in tiles], axis=0).astype(jnp.bfloat16)
-        pick_row = jnp.concatenate([jnp.where(lane == tile + half, 1.0, 0.0) for tile in tiles], axis=0).astype(jnp.bfloat16)
-        loads[6].wait()
-        spreads[z] = (spread_own[...] * LEVELS + 0.5).astype(jnp.int32).astype(jnp.int16)
+        picks[home] = jnp.where(lane < half, chosen * unit, chosen).astype(jnp.bfloat16)
 
     with jax.named_scope("entry_barrier"):
         pl.semaphore_wait(barrier, len(partners))
@@ -226,6 +223,9 @@
     for to_g, to_y in across:
         send(home, (to_g, index(z, to_y, core)))
     send_core(home)
+    with jax.named_scope("spread_levels"):
+        loads[6].wait()
+        spreads[z] = (spread_own[...] * LEVELS + 0.5).astype(jnp.int32).astype(jnp.int16)
     table_copies = []
     for k, to in enumerate(send_z):
         for which, (source, landing) in enumerate(((travel_ref, travels), (spreads.at[z], spreads))):
@@ -240,6 +240,11 @@
             copy.start()
             table_copies.append(copy)
 
+    with jax.named_scope("picks"):
+        lane = lax.broadcasted_iota(jnp.int32, (rows, 2 * half), 1)
+        tiles = [index(to, y, core) for to in (*line_z, z)]
+        pick_weight = jnp.concatenate([jnp.where(lane == tile, 1.0, 0.0) for tile in tiles], axis=0).astype(jnp.bfloat16)
+        pick_row = jnp.concatenate([jnp.where(lane == tile + half, 1.0, 0.0) for tile in tiles], axis=0).astype(jnp.bfloat16)
     split(home)
     for at_g, at_y in across[::-1]:
         slot = slot_of(at_g, at_y, core)
@@ -265,7 +270,10 @@
         member = jnp.concatenate([member, member], axis=1)
         data = halves[...].reshape(2 * total, samples)
         stacks = jnp.dot(member, data, preferred_element_type=jnp.float32)
-        uppers = pltpu.roll(stacks, samples - 1, 1)
+        largest = jnp.maximum(jnp.max(jnp.abs(stacks), axis=1, keepdims=True), 1e-30)
+        uppers = largest * (1.0 / LEVELS)
+        level = jnp.round(stacks * (LEVELS / largest)).astype(jnp.int32)
+        stacks = lax.shift_left(pltpu.roll(level, samples - 1, 1), 16) + (level + 32768)
 
     part_copies = []
     with jax.named_scope("other_images"):

time: 15.9 us -> 15.7 us (0.987)
  no operation moved by 1% of the time
where the time goes in v5:
time: 15.7 us; the launch traced here: 15.6 us
  Pallas kernels  15 us (96%)
  local copies, waits for them, and re-layouts  0.58 us (4%)
    pallas_call x1, Pallas kernels, per_device(): pl.pallas_call(functools.partial(kernel, sizes, groups, half, scale), out...  15 us
    unnamed x1, local copies, waits for them, and re-layouts  0.58 us

profile of v5, /device:TPU:0, one launch (start us, length us, event | category | flops | bytes accessed | tf_op | source)
XLA Modules:
  0.0 15.6 jit_solution(8973979735004351521)
XLA Ops:
  0.0 15.0 %shard_map.73 = f32[1,512]{1,0:T(1,128)S(1)} custom-call(s32[4,16]{1,0:T(4,128)} %bitcast.8, s32[1,16]{1,0:T(1,128)} %bitcast.11, s32[4,16]{1,0:T(4,128)} %bitcast.9, bf16[4,16]{1,0:T(4,128)(2,1)} %bitcast.10, bf16[16,1920]{1,0:T(8,128)(2,1)} %traces_ref.1, f32[16,512]{1,0:T(8,128)} %bitcast.6, f32[16,512]{1,0:T(8,128)} %bitcast.7), custom_call_target="tpu_custom_call" | custom-call | flops 100000000 | bytes 1000000 | tf_op jit(solution)/shard_map/pallas_call | solution.py:339
  15.0 0.6 %copy.9 = f32[1,512]{1,0:T(1,128)} copy(f32[1,512]{1,0:T(1,128)S(1)} %shard_map.73) | data formatting | bytes 4096

commit v6 on v5

--- a/solution.py
+++ b/solution.py
@@ -89,7 +89,7 @@
     return (2.0 * inner + both(inner, 1))[:, :samples]
 
 
-def partial_image(stack, unit, travel, spread):
+def partial_image(stack, upper, travel, spread):
     floor_value = jnp.floor(travel)
     fraction = travel - floor_value
     lower = floor_value.astype(jnp.int32)
@@ -99,18 +99,18 @@
     for c in range(travel.shape[1] // LANES):
         cells = slice(c * LANES, (c + 1) * LANES)
         here, within = chunk[:, cells], inner[:, cells]
-        pair = jnp.zeros(here.shape, jnp.int32)
+        low = jnp.zeros(here.shape, jnp.float32)
+        high = jnp.zeros(here.shape, jnp.float32)
         for k in range(stack.shape[1] // LANES):
             samples = slice(k * LANES, (k + 1) * LANES)
             mine = here == k
             picked = jnp.take_along_axis(stack[:, samples], within, axis=1, mode="promise_in_bounds")
-            pair = jnp.where(mine, picked, pair)
-        high = lax.shift_right_arithmetic(pair, 16)
-        low = (pair - lax.shift_left(high, 16)).astype(jnp.float32) - 32768.0
-        high = high.astype(jnp.float32)
+            above = jnp.take_along_axis(upper[:, samples], within, axis=1, mode="promise_in_bounds")
+            low = jnp.where(mine, picked, low)
+            high = jnp.where(mine, above, high)
         part = fraction[:, cells]
         value = spread[:, cells] * ((1.0 - part) * low + part * high)
-        pieces.append(jnp.sum(value * unit, axis=0, keepdims=True))
+        pieces.append(jnp.sum(value, axis=0, keepdims=True))
     return jnp.concatenate(pieces, axis=1)
 
 
@@ -156,7 +156,7 @@
             (travel_ref, travels.at[z]), (spread_ref, spread_own),
         ))
     ]
-    for k in (0, 1, 2, 3, 4, 6, 5):
+    for k in (4, 1, 0, 2, 3):
         loads[k].start()
 
     barrier = pltpu.get_barrier_semaphore()
@@ -180,6 +180,8 @@
         blocks[home] = levels.astype(jnp.int32).astype(jnp.int16)
         picks[home] = jnp.where(lane < half, chosen * unit, chosen).astype(jnp.bfloat16)
 
+    for k in (6, 5):
+        loads[k].start()
     with jax.named_scope("entry_barrier"):
         pl.semaphore_wait(barrier, len(partners))
 
@@ -195,7 +197,7 @@
                 device_id=to,
                 device_id_type=MESH,
             )
-            for which, landing in enumerate((picks, blocks))
+            for which, landing in enumerate((blocks, picks))
         ]
 
     def send(slot, to):
@@ -270,10 +272,7 @@
         member = jnp.concatenate([member, member], axis=1)
         data = halves[...].reshape(2 * total, samples)
         stacks = jnp.dot(member, data, preferred_element_type=jnp.float32)
-        largest = jnp.maximum(jnp.max(jnp.abs(stacks), axis=1, keepdims=True), 1e-30)
-        uppers = largest * (1.0 / LEVELS)
-        level = jnp.round(stacks * (LEVELS / largest)).astype(jnp.int32)
-        stacks = lax.shift_left(pltpu.roll(level, samples - 1, 1), 16) + (level + 32768)
+        uppers = pltpu.roll(stacks, samples - 1, 1)
 
     part_copies = []
     with jax.named_scope("other_images"):

time: 15.7 us -> 15.7 us (level)
  no operation moved by 1% of the time
where the time goes in v6:
time: 15.7 us; the launch traced here: 15.6 us
  Pallas kernels  15 us (96%)
  local copies, waits for them, and re-layouts  0.58 us (4%)
    pallas_call x1, Pallas kernels, per_device(): pl.pallas_call(functools.partial(kernel, sizes, groups, half, scale), out...  15 us
    unnamed x1, local copies, waits for them, and re-layouts  0.58 us

profile of v6, /device:TPU:0, one launch (start us, length us, event | category | flops | bytes accessed | tf_op | source)
XLA Modules:
  0.0 15.6 jit_solution(17308074155618690892)
XLA Ops:
  0.0 15.0 %shard_map.73 = f32[1,512]{1,0:T(1,128)S(1)} custom-call(s32[4,16]{1,0:T(4,128)} %bitcast.8, s32[1,16]{1,0:T(1,128)} %bitcast.11, s32[4,16]{1,0:T(4,128)} %bitcast.9, bf16[4,16]{1,0:T(4,128)(2,1)} %bitcast.10, bf16[16,1920]{1,0:T(8,128)(2,1)} %traces_ref.1, f32[16,512]{1,0:T(8,128)} %bitcast.6, f32[16,512]{1,0:T(8,128)} %bitcast.7), custom_call_target="tpu_custom_call" | custom-call | flops 100000000 | bytes 1000000 | tf_op jit(solution)/shard_map/pallas_call | solution.py:338
  15.0 0.6 %copy.9 = f32[1,512]{1,0:T(1,128)} copy(f32[1,512]{1,0:T(1,128)S(1)} %shard_map.73) | data formatting | bytes 4096
